TPU v7x, 256 devices: a whole 4x4x8 slice. The times are simulated.
256 devices in a mesh: state: 4 (over y), frame: 64 (over x, z, core).
Axes of the slice: x: 4, y: 4, z: 8, core: 2. Of those that a mesh axis runs over, the one named last changes fastest.
Arguments:
- energies: float32 [512, 524288], P('state', 'frame'), may hold values from -195 to 215, as said below
- sample_counts: int32 [512], P('state'), may hold values from 1 to 4096, 524288 in all
- state_leg: int32 [512], P('state'), may hold values from 0 to 7, never falling along the last dimension, each value on 1 to 128 neighbouring positions
- bin_index: int32 [524288, 6, 8], P('frame'), may hold values from 0 to 255
Outputs:
- rdf: float32 [1536, 512], P('frame', 'state')
- leg_free: float32 [512], P('state')
Inputs may be any that keep to these rules, and one draw needn't show every extreme that they name: The energies of the shown and hidden draws lie in this range. `sample_counts`: the counts sum to 524288. `state_leg`: each group is a nonempty run of consecutive states, numbered in order.
All inputs are finite; a program needn't handle non-finite values. No bound on the sum of `sample_counts` on one device may be relied on, other than what follows from the above.
Results may differ from a plain program's by a relative error of at most 0.0003.
Values sent between devices are 32-bit elements; how exact they have to be, the bound alone decides.
A program may use at most 64 MiB of HBM per device.

v0:
```python
import jax
import jax.numpy as jnp
from jax import lax
from jax.sharding import PartitionSpec as P

BINS = 256
TYPES = 6
PAIRS = 8
LEGS = 8
ITERS = 2


def denominator(energies, log_counts, free_energy):
    scores = (log_counts + free_energy)[:, None] - energies
    largest = jnp.max(scores, axis=0)
    largest = lax.pmax(largest, "state")
    totals = lax.psum(jnp.sum(jnp.exp(scores - largest[None, :]), axis=0), "state")
    return largest + jnp.log(totals)


def frame_lse(scores):
    largest = jnp.max(scores, axis=1)
    largest = lax.pmax(largest, "frame")
    totals = lax.psum(jnp.sum(jnp.exp(scores - largest[:, None]), axis=1), "frame")
    return largest + jnp.log(totals)


def local(energies, sample_counts, state_leg, bin_index):
    state_rows = energies.shape[0]
    frame_cols = energies.shape[1]
    log_counts = jnp.log(sample_counts.astype(jnp.float32))
    free_energy = jnp.zeros((state_rows,), jnp.float32)
    for iteration in range(ITERS):
        log_denominator = denominator(energies, log_counts, free_energy)
        free_energy = -frame_lse(-energies - log_denominator[None, :])
    final_denominator = denominator(energies, log_counts, free_energy)
    weights = jnp.exp(free_energy[:, None] - energies - final_denominator[None, :]).astype(
        jnp.bfloat16
    )
    leg_table = (state_leg[:, None] == jnp.arange(LEGS, dtype=jnp.int32)[None, :]).astype(
        jnp.float32
    )
    leg_totals, leg_sizes = lax.psum(
        (jnp.sum(leg_table * free_energy[:, None], axis=0), jnp.sum(leg_table, axis=0)), "state"
    )
    leg_mean = leg_totals / leg_sizes
    leg_free = free_energy - jnp.sum(leg_table * leg_mean[None, :], axis=1)
    block = min(1024, frame_cols)
    columns = TYPES * BINS
    own_rows = columns // lax.axis_size("frame")
    bin_range = jnp.arange(BINS, dtype=jnp.int32)

    def add_block(index, total):
        rows = lax.dynamic_slice_in_dim(bin_index, index * block, block, 0)
        weight_block = lax.dynamic_slice_in_dim(weights, index * block, block, 1)
        counted = jnp.zeros((block, TYPES, BINS), jnp.int32)
        for pair in range(PAIRS):
            counted = counted + (rows[:, :, pair, None] == bin_range[None, None, :]).astype(
                jnp.int32
            )
        counted = counted.reshape(block, columns).astype(jnp.bfloat16)
        return total + lax.dot_general(
            counted, weight_block, (((0,), (1,)), ((), ())), preferred_element_type=jnp.float32
        )

    summed = lax.psum(
        lax.fori_loop(
            0, frame_cols // block, add_block, jnp.zeros((columns, state_rows), jnp.float32)
        ),
        "frame",
    )
    mine = lax.dynamic_slice_in_dim(summed, lax.axis_index("frame") * own_rows, own_rows, 0)
    rdf = mine * (BINS / PAIRS)
    return (rdf, leg_free)


def solution(mesh):
    placed = (P("state", "frame"), P("state"), P("state"), P("frame", None, None))
    return jax.shard_map(
        local,
        mesh=mesh,
        in_specs=placed,
        out_specs=(P("frame", "state"), P("state")),
        check_vma=False,
    )
```

profile of v0, /device:TPU:1, one launch (start us, length us, event | category | flops | bytes accessed | tf_op | source)
XLA Modules:
  0.0 891.3 jit_solution(5436173738501284529)
XLA Ops:
  10.5 14.4 %pmax.35 = f32[8192]{0:T(1024)S(1)} all-reduce(f32[8192]{0:T(1024)S(1)} %subtract_reduce_fusion.4), channel_id=1, replica_groups=mesh['state'=4,'frame'=64] {'state'}, use_global_device_ids=true, to_apply=%region_1.0 | all-reduce | flops 8192 | bytes 65536 | tf_op jit(solution)/shard_map/pmax | solution.py:16
  24.9 3.0 exponential_reduce_fusion.4
  27.9 10.9 %psum.56 = f32[8192]{0:T(1024)S(1)} all-reduce(f32[8192]{0:T(1024)S(1)} %exponential_reduce_fusion.4), channel_id=1, replica_groups=mesh['state'=4,'frame'=64] {'state'}, use_global_device_ids=true, to_apply=%region_3.0 | all-reduce | flops 8192 | bytes 65536 | tf_op jit(solution)/shard_map/psum | solution.py:17
  41.6 134.4 %pmax.36 = f32[128]{0:T(128)S(1)} all-reduce(f32[128]{0:T(128)S(1)} %subtract_reduce_fusion.3), channel_id=1, replica_groups=mesh['state'=4,'frame'=64] {'frame'}, use_global_device_ids=true, to_apply=%region_5.0 | all-reduce | flops 128 | bytes 1024 | tf_op jit(solution)/shard_map/pmax | solution.py:23
  176.0 3.2 exponential_reduce_fusion.3
  179.2 123.6 %psum.57 = f32[128]{0:T(128)S(1)} all-reduce(f32[128]{0:T(128)S(1)} %exponential_reduce_fusion.3), channel_id=1, replica_groups=mesh['state'=4,'frame'=64] {'frame'}, use_global_device_ids=true, to_apply=%region_7.0 | all-reduce | flops 128 | bytes 1024 | tf_op jit(solution)/shard_map/psum | solution.py:24
  305.3 12.5 %pmax.37 = f32[8192]{0:T(1024)S(1)} all-reduce(f32[8192]{0:T(1024)S(1)} %subtract_reduce_fusion.2), channel_id=1, replica_groups=mesh['state'=4,'frame'=64] {'state'}, use_global_device_ids=true, to_apply=%region_9.0 | all-reduce | flops 8192 | bytes 65536 | tf_op jit(solution)/shard_map/pmax | solution.py:16
  320.8 11.0 %psum.58 = f32[8192]{0:T(1024)S(1)} all-reduce(f32[8192]{0:T(1024)S(1)} %exponential_reduce_fusion.2), channel_id=1, replica_groups=mesh['state'=4,'frame'=64] {'state'}, use_global_device_ids=true, to_apply=%region_11.0 | all-reduce | flops 8192 | bytes 65536 | tf_op jit(solution)/shard_map/psum | solution.py:17
  334.5 131.6 %pmax.38 = f32[128]{0:T(128)S(1)} all-reduce(f32[128]{0:T(128)S(1)} %subtract_reduce_fusion.1), channel_id=1, replica_groups=mesh['state'=4,'frame'=64] {'frame'}, use_global_device_ids=true, to_apply=%region_13.0 | all-reduce | flops 128 | bytes 1024 | tf_op jit(solution)/shard_map/pmax | solution.py:23
  466.1 3.2 exponential_reduce_fusion.1
  469.3 124.0 %psum.59 = f32[128]{0:T(128)S(1)} all-reduce(f32[128]{0:T(128)S(1)} %exponential_reduce_fusion.1), channel_id=1, replica_groups=mesh['state'=4,'frame'=64] {'frame'}, use_global_device_ids=true, to_apply=%region_15.0 | all-reduce | flops 128 | bytes 1024 | tf_op jit(solution)/shard_map/psum | solution.py:24
  595.9 12.4 %pmax.39 = f32[8192]{0:T(1024)S(1)} all-reduce(f32[8192]{0:T(1024)S(1)} %subtract_reduce_fusion), channel_id=1, replica_groups=mesh['state'=4,'frame'=64] {'state'}, use_global_device_ids=true, to_apply=%region_17.0 | all-reduce | flops 8192 | bytes 65536 | tf_op jit(solution)/shard_map/pmax | solution.py:16
  608.4 3.0 exponential_reduce_fusion
  611.5 11.4 %all-reduce = (f32[8192]{0:T(1024)S(1)}, f32[8]{0:T(128)S(1)}, f32[8]{0:T(128)S(1)}) all-reduce(f32[8192]{0:T(1024)S(1)} %exponential_reduce_fusion, f32[8]{0:T(128)S(1)} %get-tuple-element.164, f32[8]{0:T(128)S(1)} %get-tuple-element.163), channel_id=1, replica_groups=mesh['state'=4,'frame'=64] {'state'}, use_global_device_ids=true, to_apply=%region_19.0 | all-reduce | flops 8208 | bytes 65664 | tf_op jit(solution)/shard_map/psum | solution.py:17
  625.8 74.5 %while.15 = (s32[]{:T(128)}, f32[1536,128]{1,0:T(8,128)S(1)}, s32[8192,6,8]{0,2,1:T(8,128)}, bf16[128,8192]{1,0:T(8,128)(2,1)S(1)}, s32[]{:T(128)}, /*index=5*/s...) while((s32[]{:T(128)}, f32[1536,128]{1,0:T(8,128)S(1)}, ...), condition=%wide.region_21.0_spmd.clone.clone, body=%wide.region_20.0_spmd.clone.clone.sunk | while | flops 440795136 | bytes 9134405 | solution.py:67
  628.3 5.7 add_convert_fusion.2
  637.2 5.7 add_convert_fusion.2
  646.6 5.7 add_convert_fusion.2
  656.2 5.7 add_convert_fusion.2
  665.6 5.7 add_convert_fusion.2
  674.8 5.7 add_convert_fusion.2
  684.0 5.7 add_convert_fusion.2
  693.5 5.7 add_convert_fusion.2
  701.9 181.2 %all-reduce.3.cloned.1.call-done = f32[1536,128]{1,0:T(8,128)} async-done(((f32[1536,128]{1,0:T(8,128)}), f32[1536,128]{1,0:T(8,128)}) %all-reduce.3.cloned.1.call-update) | async-done | bytes 786448 | tf_op jit(solution)/shard_map/psum | solution.py:66
  (91 shorter events, 50.9 us)
Async XLA Ops:
  7.2 876.0 %all-reduce.3.cloned.1.call-start = ((), (), s32[]{:S(2)}) async-start(), calls=%async_computation | async-start | bytes 1572864 | tf_op jit(solution)/shard_map/psum | solution.py:66
  38.9 263.9 %copy-start.1 = (s32[128]{0:T(128)S(1)}, s32[128]{0:T(128)}, u32[]{:S(2)}) copy-start(s32[128]{0:T(128)} %param.7) | copy-start | bytes 1540
  593.3 18.1 %copy-start.2 = (s32[128]{0:T(128)S(1)}, s32[128]{0:T(128)}, u32[]{:S(2)}) copy-start(s32[128]{0:T(128)} %param.8) | copy-start | bytes 1540
  700.4 0.9 copy-start
Sparse Core Ops, SparseCore 0:
  701.4 181.6 all-reduce.2
where the time goes:
time: 893 us; the launch traced here: 891 us
  blocking collectives  586 us (66%)
  waiting for transfers between devices  181 us (20%)
  other arithmetic  79.9 us (9%)
  local copies, waits for them, and re-layouts  20.4 us (2%)
  between operations  14.2 us (2%)
    pmax x2, blocking collectives, frame_lse(): largest = lax.pmax(largest, 'frame')  266 us
    psum x2, blocking collectives, frame_lse(): lax.psum(jnp.sum(jnp.exp(scores - largest[:, None]), axis=1), 'frame')  248 us
    psum x1, waiting for transfers between devices, local(): lax.psum(lax.fori_loop(0, frame_cols // block, add_block, jnp.zeros((colu...  181 us
    convert_element_type x8, other arithmetic, add_block(): counted = counted.reshape(block, columns).astype(jnp.bfloat16)  45.7 us
    pmax x3, blocking collectives, denominator(): largest = lax.pmax(largest, 'state')  39.3 us
    psum x3, blocking collectives, denominator(): lax.psum(jnp.sum(jnp.exp(scores - largest[None, :]), axis=0), 'state')  33.3 us
    slice x8, local copies, waits for them, and re-layouts, add_block(): rows[:, :, pair, None] == bin_range[None, None, :]  18.9 us
  transfers between devices with their start and end apart: 1, of which 1 were waited for; matrix products, arithmetic and copies ran while one was open for 0% of the time, Pallas kernels for 0%

commit v1 on v0

v1 whole, which is shorter than its diff:
```python
import functools

import jax
import jax.numpy as jnp
from jax import lax
from jax.experimental import pallas as pl
from jax.experimental.pallas import tpu as pltpu
from jax.sharding import PartitionSpec as P

BINS = 256
TYPES = 6
PAIRS = 8
LEGS = 8
ITERS = 2
YS = 4
XS = 4
ZS = 8
FS = XS * ZS * 2
LANES = 128
ROWS = 128
COLS = 8192
BLOCKS = COLS // LANES
OWN = TYPES * BINS // FS
PARTS = 4
WIDE = 256
MESH = pl.DeviceIdType.MESH


def eye():
    shape = (ROWS, LANES)
    return lax.broadcasted_iota(jnp.int32, shape, 0) == lax.broadcasted_iota(jnp.int32, shape, 1)


def to_col(row):
    return jnp.sum(jnp.where(eye(), jnp.broadcast_to(row, (ROWS, LANES)), 0.0), axis=1, keepdims=True)


def to_row(col):
    return jnp.sum(jnp.where(eye(), jnp.broadcast_to(col, (ROWS, LANES)), 0.0), axis=0, keepdims=True)


def place(row):
    group, rest = divmod(row, 2 * OWN)
    x, z = divmod(group, ZS)
    return z * (XS * 2 * OWN) + x * 2 * OWN + rest


def count_block(bins, counts, block):
    cols = pl.ds(pl.multiple_of(block * WIDE, WIDE), WIDE)
    iota = lax.broadcasted_iota(jnp.int32, (16, WIDE), 0)
    for t in range(TYPES):
        rows = bins[t, :, cols]
        low = rows & 15
        one = jnp.left_shift(1, (rows >> 4) * 2)
        even = odd = None
        for group in ((0, 1, 2), (3, 4, 5), (6, 7)):
            word = None
            for p in group:
                hot = jnp.where(low[p : p + 1] == iota, one[p : p + 1], 0)
                word = hot if word is None else word + hot
            a = word & 0x33333333
            b = lax.shift_right_logical(word, 2) & 0x33333333
            even = a if even is None else even + a
            odd = b if odd is None else odd + b
        for half, nibbles in ((0, even), (16, odd)):
            for q in range(0, 8, 2):
                v = lax.shift_right_logical(nibbles, 4 * q) if q else nibbles
                if q < 6:
                    v = v & 255
                v = v.astype(jnp.float32).astype(jnp.bfloat16)
                upper = (v + jnp.bfloat16(2048)) - jnp.bfloat16(2048)
                base = t * BINS + 32 * q + half
                counts[pl.ds(place(base), 16), cols] = v - upper
                counts[pl.ds(place(base + 32), 16), cols] = upper * jnp.bfloat16(0.0625)


def kernel(
    e_hbm, n_ref, leg_ref, bins_hbm, out_ref, leg_out,
    energies, bins, counts, weights, acol, mbuf, sbuf, dbuf,
    ybuf, fbuf, legbuf, part, crecv, xsend, xrecv, zsend, zrecv,
    e_sem, bins_sem, ysend_sem, yrecv_sem, fsend_sem, frecv_sem, legsend_sem, legrecv_sem,
    csend_sem, crecv_sem, xsend_sem, xrecv_sem, zsend_sem, zrecv_sem,
):
    y = lax.axis_index("state")
    f = lax.axis_index("frame")
    core = lax.rem(f, 2)
    z = lax.rem(lax.div(f, 2), ZS)
    x = lax.div(f, 2 * ZS)
    width = COLS // PARTS

    loads = [
        pltpu.make_async_copy(
            e_hbm.at[:, pl.ds(i * width, width)], energies.at[:, pl.ds(i * width, width)], e_sem.at[i]
        )
        for i in range(PARTS)
    ]
    for load in loads:
        load.start()
    bins_load = pltpu.make_async_copy(bins_hbm, bins, bins_sem)
    bins_load.start()

    barrier = pltpu.get_barrier_semaphore()

    def greet(d, _):
        pl.semaphore_signal(barrier, inc=1, device_id=(y, lax.rem(f + d, FS)), device_id_type=MESH)
        return 0

    for d in range(1, YS):
        pl.semaphore_signal(barrier, inc=1, device_id=(lax.rem(y + d, YS), f), device_id_type=MESH)
    lax.fori_loop(1, FS, greet, 0)

    def count(first, last):
        def body(b, _):
            count_block(bins, counts, b)
            return 0

        lax.fori_loop(first, last, body, 0)

    def set_terms(row):
        acol[...] = jnp.broadcast_to(to_col(row), (ROWS, LANES))

    def state_pass(first, last):
        def body(j, _):
            cols = pl.ds(pl.multiple_of(j * LANES, LANES), LANES)
            scores = acol[...] - energies[:, cols]
            largest = jnp.max(scores, axis=0, keepdims=True)
            mbuf[pl.ds(j, 1), :] = largest
            sbuf[pl.ds(j, 1), :] = jnp.sum(jnp.exp(scores - largest), axis=0, keepdims=True)
            return 0

        lax.fori_loop(first, last, body, 0, unroll=2)

    def y_copy(stage, d):
        return pltpu.make_async_remote_copy(
            src_ref=ybuf.at[stage, y], dst_ref=ybuf.at[stage, y],
            send_sem=ysend_sem.at[stage], recv_sem=yrecv_sem.at[stage],
            device_id=(lax.rem(y + d, YS), f), device_id_type=MESH,
        )

    def y_start(stage):
        ybuf[stage, y] = mbuf[...] + jnp.log(sbuf[...])

    def y_send(stage):
        for d in (2, 1, 3):
            y_copy(stage, d).start()

    def y_finish(stage):
        got = ybuf.at[stage, pl.ds(0, YS - 1)]
        pltpu.make_async_copy(got, got, yrecv_sem.at[stage]).wait()
        parts = [ybuf[stage, k] for k in range(YS)]
        largest = functools.reduce(jnp.maximum, parts)
        total = functools.reduce(jnp.add, [jnp.exp(part - largest) for part in parts])
        dbuf[...] = largest + jnp.log(total)

    def frame_pass(stage):
        def smallest(j, least):
            cols = pl.ds(pl.multiple_of(j * LANES, LANES), LANES)
            return jnp.minimum(least, energies[:, cols] + dbuf[pl.ds(j, 1), :])

        least = lax.fori_loop(
            0, BLOCKS, smallest, jnp.full((ROWS, LANES), jnp.inf, jnp.float32), unroll=2
        )
        least = jnp.min(least, axis=1, keepdims=True)
        acol[...] = jnp.broadcast_to(least, (ROWS, LANES))

        def add(j, total):
            cols = pl.ds(pl.multiple_of(j * LANES, LANES), LANES)
            return total + jnp.exp(acol[...] - (energies[:, cols] + dbuf[pl.ds(j, 1), :]))

        total = lax.fori_loop(0, BLOCKS, add, jnp.zeros((ROWS, LANES), jnp.float32), unroll=2)
        total = jnp.sum(total, axis=1, keepdims=True)
        fbuf[stage, f] = to_row(jnp.log(total) - least)

    def f_send(stage):
        def start(d, _):
            pltpu.make_async_remote_copy(
                src_ref=fbuf.at[stage, f], dst_ref=fbuf.at[stage, f],
                send_sem=fsend_sem.at[stage], recv_sem=frecv_sem.at[stage],
                device_id=(y, lax.rem(f + d, FS)), device_id_type=MESH,
            ).start()
            return 0

        lax.fori_loop(1, FS, start, 0)

    def f_finish(stage):
        got = fbuf.at[stage, pl.ds(0, FS - 1)]
        pltpu.make_async_copy(got, got, frecv_sem.at[stage]).wait()
        parts = fbuf[stage]
        largest = jnp.max(parts, axis=0)
        return -(largest + jnp.log(jnp.sum(jnp.exp(parts - largest[None]), axis=0)))

    log_counts = jnp.log(n_ref[...].astype(jnp.float32))
    set_terms(log_counts)
    for i in range(PARTS):
        loads[i].wait()
        state_pass(i * BLOCKS // PARTS, (i + 1) * BLOCKS // PARTS)
    y_start(0)
    bins_load.wait()
    blocks = COLS // WIDE
    count(0, blocks // 4)
    pl.semaphore_wait(barrier, YS - 1 + FS - 1)
    y_send(0)
    count(blocks // 4, blocks // 2)
    y_finish(0)
    frame_pass(0)
    f_send(0)
    count(blocks // 2, blocks)
    free = f_finish(0)

    set_terms(log_counts + free)
    state_pass(0, BLOCKS)
    y_start(1)
    y_send(1)
    y_finish(1)
    frame_pass(1)
    f_send(1)
    free = f_finish(1)

    set_terms(log_counts + free)
    state_pass(0, BLOCKS)
    y_start(2)
    y_send(2)
    free_col = to_col(free)
    leg_col = to_col(leg_ref[...].astype(jnp.float32))
    lane = lax.broadcasted_iota(jnp.int32, (ROWS, LANES), 1).astype(jnp.float32)
    table = (jnp.broadcast_to(leg_col, (ROWS, LANES)) == lane).astype(jnp.float32)
    legbuf[y, 0:1] = jnp.sum(table * free_col, axis=0, keepdims=True)
    legbuf[y, 1:2] = jnp.sum(table, axis=0, keepdims=True)
    for d in range(1, YS):
        pltpu.make_async_remote_copy(
            src_ref=legbuf.at[y], dst_ref=legbuf.at[y],
            send_sem=legsend_sem, recv_sem=legrecv_sem,
            device_id=(lax.rem(y + d, YS), f), device_id_type=MESH,
        ).start()
    acol[...] = jnp.broadcast_to(free_col, (ROWS, LANES))
    y_finish(2)

    def weigh(j, _):
        cols = pl.ds(pl.multiple_of(j * LANES, LANES), LANES)
        value = jnp.exp((acol[...] - energies[:, cols]) - dbuf[pl.ds(j, 1), :])
        weights[:, cols] = value.astype(jnp.bfloat16)
        return 0

    lax.fori_loop(0, BLOCKS, weigh, 0, unroll=2)

    def offset(s):
        return 4 + (1 - 2 * lax.rem(s, 2)) * lax.div(s + 1, 2)

    def core_copy(s):
        other = 1 - core
        return pltpu.make_async_remote_copy(
            src_ref=part.at[s, :, other], dst_ref=crecv.at[s],
            send_sem=csend_sem, recv_sem=crecv_sem.at[s],
            device_id=(y, f + 1 - 2 * core), device_id_type=MESH,
        )

    def x_copy(s, d):
        to = lax.rem(x + d, XS)
        return pltpu.make_async_remote_copy(
            src_ref=xsend.at[s, to], dst_ref=xrecv.at[s, d - 1],
            send_sem=xsend_sem, recv_sem=xrecv_sem.at[s],
            device_id=(y, to * (2 * ZS) + z * 2 + core), device_id_type=MESH,
        )

    def z_copy(s):
        to = lax.rem(z + offset(s), ZS)
        return pltpu.make_async_remote_copy(
            src_ref=zsend.at[s], dst_ref=zrecv.at[s],
            send_sem=zsend_sem, recv_sem=zrecv_sem,
            device_id=(y, x * (2 * ZS) + to * 2 + core), device_id_type=MESH,
        )

    def core_post(s):
        pltpu.make_async_copy(crecv.at[s], crecv.at[s], crecv_sem.at[s]).wait()
        xsend[s] = part[s, :, core] + crecv[s]
        for d in (2, 1, 3):
            x_copy(s, d).start()

    def x_post(s):
        pltpu.make_async_copy(xrecv.at[s], xrecv.at[s], xrecv_sem.at[s]).wait()
        zsend[s] = (xsend[s, x] + xrecv[s, 0]) + (xrecv[s, 1] + xrecv[s, 2])

    def x_post_send(s):
        x_post(s)
        z_copy(s).start()

    lag = 5

    def step(s, _):
        rows = pl.ds(pl.multiple_of(lax.rem(z + offset(s), ZS) * (XS * 2 * OWN), 32), XS * 2 * OWN)
        result = lax.dot_general(
            counts[rows, :], weights[...], (((1,), (1,)), ((), ())), preferred_element_type=jnp.float32
        )
        part[s] = result.reshape(XS, 2, OWN, LANES)
        core_copy(s).start()

        @pl.when(s >= 1)
        def _():
            core_post(s - 1)

        @pl.when(s >= lag)
        def _():
            x_post_send(s - lag)

        return 0

    lax.fori_loop(0, ZS, step, 0)
    core_post(ZS - 1)

    got = legbuf.at[pl.ds(0, YS - 1)]
    pltpu.make_async_copy(got, got, legrecv_sem).wait()
    legs = (legbuf[0] + legbuf[1]) + (legbuf[2] + legbuf[3])
    leg_mean = legs[0:1] / jnp.maximum(legs[1:2], 1.0)
    leg_out[...] = to_row(
        acol[:, 0:1] - jnp.sum(table * jnp.broadcast_to(leg_mean, (ROWS, LANES)), axis=1, keepdims=True)
    )

    def late(s, _):
        x_post_send(s)
        return 0

    lax.fori_loop(ZS - lag, ZS - 1, late, 0)
    x_post(ZS - 1)
    got = zrecv.at[pl.ds(0, ZS - 1)]
    pltpu.make_async_copy(got, got, zrecv_sem).wait()
    total = zsend[ZS - 1]
    for s in range(ZS - 1):
        total = total + zrecv[s]
    out_ref[...] = total * (BINS / PAIRS)

    for stage in range(ITERS + 1):
        sent = ybuf.at[stage, pl.ds(0, YS - 1)]
        pltpu.make_async_copy(sent, sent, ysend_sem.at[stage]).wait()
    for stage in range(ITERS):
        sent = fbuf.at[stage, pl.ds(0, FS - 1)]
        pltpu.make_async_copy(sent, sent, fsend_sem.at[stage]).wait()
    sent = legbuf.at[pl.ds(0, YS - 1)]
    pltpu.make_async_copy(sent, sent, legsend_sem).wait()
    pltpu.make_async_copy(crecv, crecv, csend_sem).wait()
    pltpu.make_async_copy(xrecv, xrecv, xsend_sem).wait()
    sent = zrecv.at[pl.ds(0, ZS - 1)]
    pltpu.make_async_copy(sent, sent, zsend_sem).wait()


def local(energies, sample_counts, state_leg, bin_index):
    hbm = pl.BlockSpec(memory_space=pl.ANY)
    vmem = pl.BlockSpec(memory_space=pltpu.VMEM)
    f32 = jnp.float32
    dma = pltpu.SemaphoreType.DMA
    rdf, leg_free = pl.pallas_call(
        kernel,
        out_shape=(
            jax.ShapeDtypeStruct((OWN, LANES), f32),
            jax.ShapeDtypeStruct((1, LANES), f32),
        ),
        in_specs=[hbm, vmem, vmem, hbm],
        out_specs=(vmem, vmem),
        scratch_shapes=[
            pltpu.VMEM((ROWS, COLS), f32),
            pltpu.VMEM((TYPES, PAIRS, COLS), jnp.int32),
            pltpu.VMEM((TYPES * BINS, COLS), jnp.bfloat16),
            pltpu.VMEM((ROWS, COLS), jnp.bfloat16),
            pltpu.VMEM((ROWS, LANES), f32),
            pltpu.VMEM((BLOCKS, LANES), f32),
            pltpu.VMEM((BLOCKS, LANES), f32),
            pltpu.VMEM((BLOCKS, LANES), f32),
            pltpu.VMEM((ITERS + 1, YS, BLOCKS, LANES), f32),
            pltpu.VMEM((ITERS, FS, 1, LANES), f32),
            pltpu.VMEM((YS, 2, LANES), f32),
            pltpu.VMEM((ZS, XS, 2, OWN, LANES), f32),
            pltpu.VMEM((ZS, XS, OWN, LANES), f32),
            pltpu.VMEM((ZS, XS, OWN, LANES), f32),
            pltpu.VMEM((ZS, XS - 1, OWN, LANES), f32),
            pltpu.VMEM((ZS, OWN, LANES), f32),
            pltpu.VMEM((ZS, OWN, LANES), f32),
            dma((PARTS,)),
            dma,
            dma((ITERS + 1,)),
            dma((ITERS + 1,)),
            dma((ITERS,)),
            dma((ITERS,)),
            dma,
            dma,
            dma,
            dma((ZS,)),
            dma,
            dma((ZS,)),
            dma,
            dma,
        ],
        compiler_params=pltpu.CompilerParams(
            collective_id=0, has_side_effects=True, vmem_limit_bytes=56 * 2**20
        ),
        name="reweight",
    )(
        energies,
        sample_counts.reshape(1, LANES),
        state_leg.reshape(1, LANES),
        jnp.transpose(bin_index, (1, 2, 0)),
    )
    return rdf, leg_free.reshape(LANES)


def solution(mesh):
    placed = (P("state", "frame"), P("state"), P("state"), P("frame", None, None))
    return jax.shard_map(
        local,
        mesh=mesh,
        in_specs=placed,
        out_specs=(P("frame", "state"), P("state")),
        check_vma=False,
    )
```

time: 893 us -> 65.3 us (0.07)
  blocking collectives: 586 us -> 0 us
  waiting for transfers between devices: 181 us -> 0 us
  other arithmetic: 79.9 us -> 0 us
  Pallas kernels: 0 us -> 62 us
  local copies, waits for them, and re-layouts: 20.4 us -> 2.44 us
  between operations: 14.2 us -> 0.64 us
    pmax x5 -> x0, blocking collectives: 305 us -> none  [the longest x2 266 us: frame_lse(): largest = lax.pmax(largest, 'frame')]
    psum x5 -> x0, blocking collectives: 281 us -> none  [the longest x2 248 us: frame_lse(): lax.psum(jnp.sum(jnp.exp(scores - largest[:, None]), axis=1), 'frame')]
    psum x1 -> x0, waiting for transfers between devices: 181 us -> none  [local(): lax.psum(lax.fori_loop(0, frame_cols // block, add_block, jnp.zeros((colu...]
    pallas_call x0 -> x1, Pallas kernels: none -> 62 us  [local(): pl.pallas_call(kernel, out_shape=(jax.ShapeDtypeStruct((OWN, LANES), f32)...]
    convert_element_type x9 -> x0, other arithmetic: 48.6 us -> none  [the longest x8 45.7 us: add_block(): counted = counted.reshape(block, columns).astype(jnp.bfloat16)]
    slice x8 -> x0, local copies, waits for them, and re-layouts: 18.9 us -> none  [add_block(): rows[:, :, pair, None] == bin_range[None, None, :]]
    reduce_sum x7 -> x0, other arithmetic: 15.6 us -> none  [the longest x3 8.98 us: denominator(): jnp.sum(jnp.exp(scores - largest[None, :]), axis=0)]
    reduce_max x5 -> x0, other arithmetic: 13.1 us -> none  [the longest x3 7.76 us: denominator(): largest = jnp.max(scores, axis=0)]
  transfers between devices with their start and end apart: 1 -> 0, of which waited for: 1 -> 0; matrix products, arithmetic and copies ran while one was open for 0% -> 0% of each run, Pallas kernels for 0% -> 0%
where the time goes in v1:
time: 65.3 us; the launch traced here: 65.1 us
  Pallas kernels  62 us (95%)
  local copies, waits for them, and re-layouts  2.44 us (4%)
    pallas_call x1, Pallas kernels, local(): pl.pallas_call(kernel, out_shape=(jax.ShapeDtypeStruct((OWN, LANES), f32)...  62 us
    unnamed x2, local copies, waits for them, and re-layouts  2.44 us

profile of v1, /device:TPU:1, one launch (start us, length us, event | category | flops | bytes accessed | tf_op | source)
XLA Modules:
  0.0 65.1 jit_solution(9998233485710609573)
XLA Ops:
  0.6 62.0 %reweight.1 = (f32[24,128]{1,0:T(8,128)}, f32[1,128]{1,0:T(1,128)}) custom-call(f32[128,8192]{1,0:T(8,128)} %e_hbm.1, s32[1,128]{1,0:T(1,128)} %bitcast.5, s32[1,128]{1,0:T(1,128)} %bitcast.6, s32[6,8,8192]{2,1,0:T(8,128)} %bitcast.4), custom_call_target="tpu_custom_call" | custom-call | tf_op jit(solution)/shard_map/reweight/pallas_call | solution.py:350
  62.6 1.3 %copy.8 = f32[24,128]{1,0:T(8,128)} copy(f32[24,128]{1,0:T(8,128)} %get-tuple-element.8) | data formatting | bytes 24576
  63.9 1.1 %copy.9 = f32[128]{0:T(128)} copy(f32[128]{0:T(128)} %bitcast.7) | data formatting | bytes 1024

commit v2 on v1

v2 whole, which is shorter than its diff:
```python
import functools

import jax
import jax.numpy as jnp
from jax import lax
from jax.experimental import pallas as pl
from jax.experimental.pallas import tpu as pltpu
from jax.sharding import PartitionSpec as P

BINS = 256
TYPES = 6
PAIRS = 8
LEGS = 8
ITERS = 2
YS = 4
XS = 4
ZS = 8
FS = XS * ZS * 2
LANES = 128
ROWS = 128
COLS = 8192
BLOCKS = COLS // LANES
OWN = TYPES * BINS // FS
PARTS = 4
GROUPS = ROWS // 8
WIDE = 256
LOG2E = 1.4426950408889634
LN2 = 0.6931471805599453
UNROLL = 4
FAR = 3
MESH = pl.DeviceIdType.MESH


def eye():
    shape = (ROWS, LANES)
    return lax.broadcasted_iota(jnp.int32, shape, 0) == lax.broadcasted_iota(jnp.int32, shape, 1)


def to_col(row):
    return jnp.sum(jnp.where(eye(), jnp.broadcast_to(row, (ROWS, LANES)), 0.0), axis=1, keepdims=True)


def to_row(col):
    return jnp.sum(jnp.where(eye(), jnp.broadcast_to(col, (ROWS, LANES)), 0.0), axis=0, keepdims=True)


def place(row):
    group, rest = divmod(row, 2 * OWN)
    x, z = divmod(group, ZS)
    return z * (XS * 2 * OWN) + x * 2 * OWN + rest


def count_block(bins, counts, block):
    cols = pl.ds(pl.multiple_of(block * WIDE, WIDE), WIDE)
    iota = lax.broadcasted_iota(jnp.int32, (16, WIDE), 0)
    for t in range(TYPES):
        rows = bins[t, :, cols]
        low = rows & 15
        one = jnp.left_shift(1, (rows >> 4) * 2)
        even = odd = None
        for group in ((0, 1, 2), (3, 4, 5), (6, 7)):
            word = None
            for p in group:
                hot = jnp.where(low[p : p + 1] == iota, one[p : p + 1], 0)
                word = hot if word is None else word + hot
            a = word & 0x33333333
            b = lax.shift_right_logical(word, 2) & 0x33333333
            even = a if even is None else even + a
            odd = b if odd is None else odd + b
        for half, nibbles in ((0, even), (16, odd)):
            for q in range(0, 8, 2):
                v = lax.shift_right_logical(nibbles, 4 * q) if q else nibbles
                if q < 6:
                    v = v & 255
                v = v.astype(jnp.float32).astype(jnp.bfloat16)
                upper = (v + jnp.bfloat16(2048)) - jnp.bfloat16(2048)
                base = t * BINS + 32 * q + half
                counts[pl.ds(place(base), 16), cols] = v - upper
                counts[pl.ds(place(base + 32), 16), cols] = upper * jnp.bfloat16(0.0625)


def folded(value, op):
    parts = [value[8 * g : 8 * g + 8] for g in range(GROUPS)]
    while len(parts) > 1:
        parts = [op(parts[i], parts[i + 1]) for i in range(0, len(parts), 2)]
    return parts[0]


def kernel(
    e_hbm, n_ref, leg_ref, bins_hbm, out_ref,
    energies, bins, counts, weights, fold, mbuf, dbuf,
    ybuf, fbuf, legbuf, part, crecv, xsend, xrecv, drecv, zsend, zrecv,
    e_sem, bins_sem, ysend_sem, yrecv_sem, fsend_sem, frecv_sem, legsend_sem, legrecv_sem,
    csend_sem, crecv_sem, xsend_sem, xrecv_sem, dsend_sem, drecv_sem, zsend_sem, zrecv_sem,
):
    y = lax.axis_index("state")
    f = lax.axis_index("frame")
    core = lax.rem(f, 2)
    z = lax.rem(lax.div(f, 2), ZS)
    x = lax.div(f, 2 * ZS)
    width = COLS // PARTS

    loads = [
        pltpu.make_async_copy(
            e_hbm.at[:, pl.ds(i * width, width)], energies.at[:, pl.ds(i * width, width)], e_sem.at[i]
        )
        for i in range(PARTS)
    ]
    for load in loads:
        load.start()
    bins_load = pltpu.make_async_copy(bins_hbm, bins, bins_sem)
    bins_load.start()

    barrier = pltpu.get_barrier_semaphore()

    def greet(d, _):
        pl.semaphore_signal(barrier, inc=1, device_id=(y, lax.rem(f + d, FS)), device_id_type=MESH)
        return 0

    for d in range(1, YS):
        pl.semaphore_signal(barrier, inc=1, device_id=(lax.rem(y + d, YS), f), device_id_type=MESH)
    lax.fori_loop(1, FS, greet, 0)

    def count(first, last):
        def body(b, _):
            count_block(bins, counts, b)
            return 0

        lax.fori_loop(first, last, body, 0)

    def wide(col):
        return jnp.broadcast_to(col, (ROWS, LANES))

    def at(j):
        return pl.ds(pl.multiple_of(j * LANES, LANES), LANES)

    def eight(j):
        return pl.ds(pl.multiple_of(j * 8, 8), 8)

    def unfold(op):
        return functools.reduce(op, [fold[pl.ds(r, BLOCKS, stride=8), :] for r in range(8)])

    def scale_and_peak(terms, first, last):
        def body(j, _):
            e = energies[:, at(j)] * -LOG2E
            energies[:, at(j)] = e
            fold[eight(j), :] = folded(terms + e, jnp.maximum)
            return 0

        lax.fori_loop(first, last, body, 0, unroll=UNROLL)

    def peak(terms):
        def body(j, _):
            fold[eight(j), :] = folded(terms + energies[:, at(j)], jnp.maximum)
            return 0

        lax.fori_loop(0, BLOCKS, body, 0, unroll=UNROLL)

    def state_sum(terms, stage):
        mbuf[...] = unfold(jnp.maximum)

        def body(j, _):
            scores = (terms + energies[:, at(j)]) - mbuf[pl.ds(j, 1), :]
            fold[eight(j), :] = folded(jnp.exp2(scores), jnp.add)
            return 0

        lax.fori_loop(0, BLOCKS, body, 0, unroll=UNROLL)
        ybuf[stage, y] = mbuf[...] + jnp.log(unfold(jnp.add)) * LOG2E

    def y_send(stage):
        for d in (2, 1, 3):
            pltpu.make_async_remote_copy(
                src_ref=ybuf.at[stage, y], dst_ref=ybuf.at[stage, y],
                send_sem=ysend_sem.at[stage], recv_sem=yrecv_sem.at[stage],
                device_id=(lax.rem(y + d, YS), f), device_id_type=MESH,
            ).start()

    def y_finish(stage):
        got = ybuf.at[stage, pl.ds(0, YS - 1)]
        pltpu.make_async_copy(got, got, yrecv_sem.at[stage]).wait()
        parts = [ybuf[stage, k] for k in range(YS)]
        largest = functools.reduce(jnp.maximum, parts)
        total = functools.reduce(jnp.add, [jnp.exp2(part - largest) for part in parts])
        dbuf[...] = largest + jnp.log(total) * LOG2E

    def frame_sum(stage):
        def greatest(j, most):
            return jnp.maximum(most, energies[:, at(j)] - dbuf[pl.ds(j, 1), :])

        most = lax.fori_loop(
            0, BLOCKS, greatest, jnp.full((ROWS, LANES), -jnp.inf, jnp.float32), unroll=UNROLL
        )
        most = jnp.max(most, axis=1, keepdims=True)
        shift = wide(most)

        def add(j, total):
            return total + jnp.exp2((energies[:, at(j)] - dbuf[pl.ds(j, 1), :]) - shift)

        total = lax.fori_loop(0, BLOCKS, add, jnp.zeros((ROWS, LANES), jnp.float32), unroll=UNROLL)
        total = jnp.sum(total, axis=1, keepdims=True)
        fbuf[stage, f] = to_row(most) + jnp.log(to_row(total)) * LOG2E

    def hops(k):
        dx, dz, dc = k
        return min(dx, XS - dx) + min(dz, ZS - dz) + 0.5 * dc

    frame_partners = sorted(
        [(dx, dz, dc) for dx in range(XS) for dz in range(ZS) for dc in range(2)], key=hops, reverse=True
    )[:-1]
    x_at = [lax.rem(x + d, XS) * (2 * ZS) for d in range(XS)]
    z_at = [lax.rem(z + d, ZS) * 2 for d in range(ZS)]
    c_at = [core, 1 - core]

    def f_send(stage):
        for dx, dz, dc in frame_partners:
            pltpu.make_async_remote_copy(
                src_ref=fbuf.at[stage, f], dst_ref=fbuf.at[stage, f],
                send_sem=fsend_sem.at[stage], recv_sem=frecv_sem.at[stage],
                device_id=(y, x_at[dx] + z_at[dz] + c_at[dc]), device_id_type=MESH,
            ).start()

    def f_finish(stage):
        got = fbuf.at[stage, pl.ds(0, FS - 1)]
        pltpu.make_async_copy(got, got, frecv_sem.at[stage]).wait()
        parts = fbuf[stage]
        largest = jnp.max(parts, axis=0)
        return -(largest + jnp.log(jnp.sum(jnp.exp2(parts - largest[None]), axis=0)) * LOG2E)

    log_counts = jnp.log(n_ref[...].astype(jnp.float32)) * LOG2E
    terms = wide(to_col(log_counts))
    for i in range(PARTS):
        loads[i].wait()
        scale_and_peak(terms, i * BLOCKS // PARTS, (i + 1) * BLOCKS // PARTS)
    state_sum(terms, 0)
    bins_load.wait()
    blocks = COLS // WIDE
    pl.semaphore_wait(barrier, YS - 1 + FS - 1)
    y_send(0)
    count(0, blocks // 4)
    y_finish(0)
    frame_sum(0)
    f_send(0)
    count(blocks // 4, 3 * blocks // 4)
    free = f_finish(0)

    terms = wide(to_col(log_counts + free))
    peak(terms)
    state_sum(terms, 1)
    y_send(1)
    count(3 * blocks // 4, blocks)
    y_finish(1)
    frame_sum(1)
    f_send(1)
    free = f_finish(1)

    terms = wide(to_col(log_counts + free))
    peak(terms)
    state_sum(terms, 2)
    y_send(2)
    free_col = to_col(free)
    factors = wide(free_col)
    y_finish(2)

    def weigh(j, _):
        value = jnp.exp2((factors + energies[:, at(j)]) - dbuf[pl.ds(j, 1), :])
        weights[:, at(j)] = value.astype(jnp.bfloat16)
        return 0

    lax.fori_loop(0, BLOCKS, weigh, 0, unroll=UNROLL)

    def offset(s):
        return 4 + (1 - 2 * lax.rem(s, 2)) * lax.div(s + 1, 2)

    def core_copy(s):
        other = 1 - core
        return pltpu.make_async_remote_copy(
            src_ref=part.at[s, :, other], dst_ref=crecv.at[s],
            send_sem=csend_sem, recv_sem=crecv_sem.at[s],
            device_id=(y, f + 1 - 2 * core), device_id_type=MESH,
        )

    def x_copy(s, d):
        to = lax.rem(x + d, XS)
        return pltpu.make_async_remote_copy(
            src_ref=xsend.at[s, to], dst_ref=xrecv.at[s, d - 1],
            send_sem=xsend_sem, recv_sem=xrecv_sem.at[s],
            device_id=(y, to * (2 * ZS) + z * 2 + core), device_id_type=MESH,
        )

    def near_copy(s, d):
        to = lax.rem(x + d, XS)
        to_z = lax.rem(z + offset(s), ZS)
        return pltpu.make_async_remote_copy(
            src_ref=xsend.at[s, to], dst_ref=drecv.at[s - FAR, d],
            send_sem=dsend_sem, recv_sem=drecv_sem.at[s - FAR],
            device_id=(y, to * (2 * ZS) + to_z * 2 + core), device_id_type=MESH,
        )

    def z_copy(s):
        to = lax.rem(z + offset(s), ZS)
        return pltpu.make_async_remote_copy(
            src_ref=zsend.at[s], dst_ref=zrecv.at[s],
            send_sem=zsend_sem, recv_sem=zrecv_sem,
            device_id=(y, x * (2 * ZS) + to * 2 + core), device_id_type=MESH,
        )

    def core_post(s):
        pltpu.make_async_copy(crecv.at[s], crecv.at[s], crecv_sem.at[s]).wait()
        xsend[s] = part[s, :, core] + crecv[s]

    def far_post(s):
        core_post(s)
        for d in (2, 1, 3):
            x_copy(s, d).start()

    def near_post(s):
        core_post(s)
        for d in (2, 1, 3, 0):
            near_copy(s, d).start()

    def x_post(s):
        pltpu.make_async_copy(xrecv.at[s], xrecv.at[s], xrecv_sem.at[s]).wait()
        zsend[s] = (xsend[s, x] + xrecv[s, 0]) + (xrecv[s, 1] + xrecv[s, 2])
        z_copy(s).start()

    lag = 5

    def step(s, _):
        rows = pl.ds(pl.multiple_of(lax.rem(z + offset(s), ZS) * (XS * 2 * OWN), 32), XS * 2 * OWN)
        result = lax.dot_general(
            counts[rows, :], weights[...], (((1,), (1,)), ((), ())), preferred_element_type=jnp.float32
        )
        part[s] = result.reshape(XS, 2, OWN, LANES)
        core_copy(s).start()

        @pl.when(jnp.logical_and(s >= 1, s <= FAR))
        def _():
            far_post(s - 1)

        @pl.when(s > FAR)
        def _():
            near_post(s - 1)

        @pl.when(s >= lag)
        def _():
            x_post(s - lag)

        return 0

    lax.fori_loop(0, ZS, step, 0)
    last = ZS - 1
    core_post(last)
    for d in (2, 1, 3):
        near_copy(last, d).start()

    leg_col = to_col(leg_ref[...].astype(jnp.float32))
    lane = lax.broadcasted_iota(jnp.int32, (ROWS, LANES), 1).astype(jnp.float32)
    table = (wide(leg_col) == lane).astype(jnp.float32)
    legbuf[y, 0:1] = jnp.sum(table * factors, axis=0, keepdims=True)
    legbuf[y, 1:2] = jnp.sum(table, axis=0, keepdims=True)
    for d in (2, 1, 3):
        pltpu.make_async_remote_copy(
            src_ref=legbuf.at[y], dst_ref=legbuf.at[y],
            send_sem=legsend_sem, recv_sem=legrecv_sem,
            device_id=(lax.rem(y + d, YS), f), device_id_type=MESH,
        ).start()
    got = zrecv.at[pl.ds(0, FAR)]
    pltpu.make_async_copy(got, got, zrecv_sem).wait()
    total = xsend[last, x]
    for s in range(FAR):
        total = total + zrecv[s]
    for s in range(FAR, last):
        got = drecv.at[s - FAR]
        pltpu.make_async_copy(got, got, drecv_sem.at[s - FAR]).wait()
        for d in range(XS):
            total = total + drecv[s - FAR, d]
    got = drecv.at[last - FAR, pl.ds(1, XS - 1)]
    pltpu.make_async_copy(got, got, drecv_sem.at[last - FAR]).wait()
    for d in range(1, XS):
        total = total + drecv[last - FAR, d]
    out_ref[0:OWN, :] = total * (BINS / PAIRS)
    got = legbuf.at[pl.ds(0, YS - 1)]
    pltpu.make_async_copy(got, got, legrecv_sem).wait()
    legs = (legbuf[0] + legbuf[1]) + (legbuf[2] + legbuf[3])
    leg_mean = legs[0:1] / jnp.maximum(legs[1:2], 1.0)
    own_mean = jnp.sum(table * jnp.broadcast_to(leg_mean, (ROWS, LANES)), axis=1, keepdims=True)
    out_ref[OWN : OWN + 8, :] = jnp.broadcast_to(to_row((free_col - own_mean) * LN2), (8, LANES))

    for stage in range(ITERS + 1):
        sent = ybuf.at[stage, pl.ds(0, YS - 1)]
        pltpu.make_async_copy(sent, sent, ysend_sem.at[stage]).wait()
    for stage in range(ITERS):
        sent = fbuf.at[stage, pl.ds(0, FS - 1)]
        pltpu.make_async_copy(sent, sent, fsend_sem.at[stage]).wait()
    sent = legbuf.at[pl.ds(0, YS - 1)]
    pltpu.make_async_copy(sent, sent, legsend_sem).wait()
    pltpu.make_async_copy(crecv, crecv, csend_sem).wait()
    pltpu.make_async_copy(xrecv, xrecv, xsend_sem).wait()
    sent = drecv.at[pl.ds(0, last - FAR)]
    pltpu.make_async_copy(sent, sent, dsend_sem).wait()
    sent = drecv.at[last - FAR, pl.ds(1, XS - 1)]
    pltpu.make_async_copy(sent, sent, dsend_sem).wait()
    sent = zrecv.at[pl.ds(0, FAR)]
    pltpu.make_async_copy(sent, sent, zsend_sem).wait()


def split(both_ref, rdf_ref, leg_ref):
    rdf_ref[...] = both_ref[0:OWN, :]
    leg_ref[...] = both_ref[OWN : OWN + 1, :]


def local(energies, sample_counts, state_leg, bin_index):
    hbm = pl.BlockSpec(memory_space=pl.ANY)
    vmem = pl.BlockSpec(memory_space=pltpu.VMEM)
    f32 = jnp.float32
    dma = pltpu.SemaphoreType.DMA
    both = pl.pallas_call(
        kernel,
        out_shape=jax.ShapeDtypeStruct((OWN + 8, LANES), f32),
        in_specs=[hbm, vmem, vmem, hbm],
        out_specs=vmem,
        scratch_shapes=[
            pltpu.VMEM((ROWS, COLS), f32),
            pltpu.VMEM((TYPES, PAIRS, COLS), jnp.int32),
            pltpu.VMEM((TYPES * BINS, COLS), jnp.bfloat16),
            pltpu.VMEM((ROWS, COLS), jnp.bfloat16),
            pltpu.VMEM((BLOCKS * 8, LANES), f32),
            pltpu.VMEM((BLOCKS, LANES), f32),
            pltpu.VMEM((BLOCKS, LANES), f32),
            pltpu.VMEM((ITERS + 1, YS, BLOCKS, LANES), f32),
            pltpu.VMEM((ITERS, FS, 1, LANES), f32),
            pltpu.VMEM((YS, 2, LANES), f32),
            pltpu.VMEM((ZS, XS, 2, OWN, LANES), f32),
            pltpu.VMEM((ZS, XS, OWN, LANES), f32),
            pltpu.VMEM((ZS, XS, OWN, LANES), f32),
            pltpu.VMEM((FAR, XS - 1, OWN, LANES), f32),
            pltpu.VMEM((ZS - FAR, XS, OWN, LANES), f32),
            pltpu.VMEM((FAR, OWN, LANES), f32),
            pltpu.VMEM((FAR, OWN, LANES), f32),
            dma((PARTS,)),
            dma,
            dma((ITERS + 1,)),
            dma((ITERS + 1,)),
            dma((ITERS,)),
            dma((ITERS,)),
            dma,
            dma,
            dma,
            dma((ZS,)),
            dma,
            dma((FAR,)),
            dma,
            dma((ZS - FAR,)),
            dma,
            dma,
        ],
        compiler_params=pltpu.CompilerParams(
            collective_id=0, has_side_effects=True, vmem_limit_bytes=56 * 2**20
        ),
        name="reweight",
    )(
        energies,
        sample_counts.reshape(1, LANES),
        state_leg.reshape(1, LANES),
        jnp.transpose(bin_index, (1, 2, 0)),
    )
    rdf, leg_free = pl.pallas_call(
        split,
        out_shape=(jax.ShapeDtypeStruct((OWN, LANES), f32), jax.ShapeDtypeStruct((1, LANES), f32)),
        in_specs=[vmem],
        out_specs=(vmem, vmem),
        name="split",
    )(both)
    return rdf, leg_free.reshape(LANES)


def solution(mesh):
    placed = (P("state", "frame"), P("state"), P("state"), P("frame", None, None))
    return jax.shard_map(
        local,
        mesh=mesh,
        in_specs=placed,
        out_specs=(P("frame", "state"), P("state")),
        check_vma=False,
    )
```

time: 65.3 us -> 60.5 us (0.926)
  local copies, waits for them, and re-layouts: 2.44 us -> 0 us
  Pallas kernels: 62 us -> 59.6 us
    unnamed x2 -> x0, local copies, waits for them, and re-layouts: 2.44 us -> none
    pallas_call x1 -> x2, Pallas kernels: 62 us -> 59.6 us  [the longest x1 58.3 us: local(): pl.pallas_call(kernel, out_shape=jax.ShapeDtypeStruct((OWN + 8, LANES), f...]
where the time goes in v2:
time: 60.5 us; the launch traced here: 60.3 us
  Pallas kernels  59.6 us (99%)
  between operations  0.64 us (1%)
    pallas_call x1, Pallas kernels, local(): pl.pallas_call(kernel, out_shape=jax.ShapeDtypeStruct((OWN + 8, LANES), f...  58.3 us
    pallas_call x1, Pallas kernels, local(): pl.pallas_call(split, out_shape=(jax.ShapeDtypeStruct((OWN, LANES), f32),...  1.32 us

profile of v2, /device:TPU:1, one launch (start us, length us, event | category | flops | bytes accessed | tf_op | source)
XLA Modules:
  0.0 60.3 jit_solution(1408994035740148043)
XLA Ops:
  0.6 58.3 %reweight.1.both_ref = f32[32,128]{1,0:T(8,128)} custom-call(f32[128,8192]{1,0:T(8,128)} %e_hbm.1, s32[1,128]{1,0:T(1,128)} %bitcast.5, s32[1,128]{1,0:T(1,128)} %bitcast.6, s32[6,8,8192]{2,1,0:T(8,128)} %bitcast.4), custom_call_target="tpu_custom_call" | custom-call | tf_op jit(solution)/shard_map/reweight/pallas_call | solution.py:417
  59.0 1.3 %split.1 = (f32[24,128]{1,0:T(8,128)}, f32[1,128]{1,0:T(1,128)}) custom-call(f32[32,128]{1,0:T(8,128)} %reweight.1.both_ref), custom_call_target="tpu_custom_call" | custom-call | tf_op jit(solution)/shard_map/split/pallas_call | solution.py:467

commit v3 on v2

--- a/solution.py
+++ b/solution.py
@@ -27,6 +27,8 @@
 LOG2E = 1.4426950408889634
 LN2 = 0.6931471805599453
 UNROLL = 4
+HALF = BLOCKS // 2
+SPAN = 8
 FAR = 3
 MESH = pl.DeviceIdType.MESH
 
@@ -79,18 +81,21 @@
                 counts[pl.ds(place(base + 32), 16), cols] = upper * jnp.bfloat16(0.0625)
 
 
-def folded(value, op):
-    parts = [value[8 * g : 8 * g + 8] for g in range(GROUPS)]
-    while len(parts) > 1:
-        parts = [op(parts[i], parts[i + 1]) for i in range(0, len(parts), 2)]
-    return parts[0]
+def online(parts):
+    largest = functools.reduce(jnp.maximum, parts)
+    return largest, functools.reduce(jnp.add, [jnp.exp2(part - largest) for part in parts])
+
+
+def merged(pairs):
+    largest = functools.reduce(jnp.maximum, [m for m, _ in pairs])
+    return largest, functools.reduce(jnp.add, [s * jnp.exp2(m - largest) for m, s in pairs])
 
 
 def kernel(
-    e_hbm, n_ref, leg_ref, bins_hbm, out_ref,
-    energies, bins, counts, weights, fold, mbuf, dbuf,
+    e_hbm, n_hbm, leg_hbm, bins_hbm, out_ref,
+    energies, n_ref, leg_ref, bins, counts, weights, terms, state_max, state_sum, frame_max, frame_sum, dbuf,
     ybuf, fbuf, legbuf, part, crecv, xsend, xrecv, drecv, zsend, zrecv,
-    e_sem, bins_sem, ysend_sem, yrecv_sem, fsend_sem, frecv_sem, legsend_sem, legrecv_sem,
+    e_sem, small_sem, bins_sem, z_ready, xc_ready, ysend_sem, yrecv_sem, fsend_sem, frecv_sem, legsend_sem, legrecv_sem,
     csend_sem, crecv_sem, xsend_sem, xrecv_sem, dsend_sem, drecv_sem, zsend_sem, zrecv_sem,
 ):
     y = lax.axis_index("state")
@@ -99,7 +104,21 @@
     z = lax.rem(lax.div(f, 2), ZS)
     x = lax.div(f, 2 * ZS)
     width = COLS // PARTS
-
+    x_at = [lax.rem(x + d, XS) * (2 * ZS) for d in range(XS)]
+    z_at = [lax.rem(z + d, ZS) * 2 for d in range(ZS)]
+    c_at = [core, 1 - core]
+    y_near = [(lax.rem(y + d, YS), f) for d in (2, 1, 3)]
+    z_near = [(y, x_at[0] + z_at[d] + core) for d in (2, 6, 1, 7)]
+    xc_near = [
+        (y, x_at[dx] + z_at[0] + c_at[dc]) for dx, dc in ((2, 1), (2, 0), (1, 1), (3, 1), (1, 0), (3, 0), (0, 1))
+    ]
+
+    barrier = pltpu.get_barrier_semaphore()
+    for device in y_near + z_near + xc_near:
+        pl.semaphore_signal(barrier, inc=1, device_id=device, device_id_type=MESH)
+
+    n_load = pltpu.make_async_copy(n_hbm, n_ref, small_sem.at[0])
+    n_load.start()
     loads = [
         pltpu.make_async_copy(
             e_hbm.at[:, pl.ds(i * width, width)], energies.at[:, pl.ds(i * width, width)], e_sem.at[i]
@@ -110,16 +129,8 @@
         load.start()
     bins_load = pltpu.make_async_copy(bins_hbm, bins, bins_sem)
     bins_load.start()
-
-    barrier = pltpu.get_barrier_semaphore()
-
-    def greet(d, _):
-        pl.semaphore_signal(barrier, inc=1, device_id=(y, lax.rem(f + d, FS)), device_id_type=MESH)
-        return 0
-
-    for d in range(1, YS):
-        pl.semaphore_signal(barrier, inc=1, device_id=(lax.rem(y + d, YS), f), device_id_type=MESH)
-    lax.fori_loop(1, FS, greet, 0)
+    leg_load = pltpu.make_async_copy(leg_hbm, leg_ref, small_sem.at[1])
+    leg_load.start()
 
     def count(first, last):
         def body(b, _):
@@ -137,81 +148,66 @@
     def eight(j):
         return pl.ds(pl.multiple_of(j * 8, 8), 8)
 
-    def unfold(op):
-        return functools.reduce(op, [fold[pl.ds(r, BLOCKS, stride=8), :] for r in range(8)])
-
-    def scale_and_peak(terms, first, last):
-        def body(j, _):
-            e = energies[:, at(j)] * -LOG2E
-            energies[:, at(j)] = e
-            fold[eight(j), :] = folded(terms + e, jnp.maximum)
+    def state_pass(first, last, scale=False):
+        def body(k, _):
+            for u in range(SPAN):
+                j = k * SPAN + u
+                pairs = []
+                for h in range(2):
+                    scores = []
+                    for g in range(h * GROUPS // 2, (h + 1) * GROUPS // 2):
+                        rows = pl.ds(8 * g, 8)
+                        e = energies[rows, at(j)]
+                        if scale:
+                            e = e * -LOG2E
+                            energies[rows, at(j)] = e
+                        scores.append(terms[rows, :] + e)
+                    pairs.append(online(scores))
+                state_max[eight(j), :], state_sum[eight(j), :] = merged(pairs)
             return 0
 
-        lax.fori_loop(first, last, body, 0, unroll=UNROLL)
-
-    def peak(terms):
-        def body(j, _):
-            fold[eight(j), :] = folded(terms + energies[:, at(j)], jnp.maximum)
+        lax.fori_loop(first // SPAN, last // SPAN, body, 0)
+
+    def y_send(stage, half):
+        rows = [pl.ds(half * HALF * 8 + r, HALF, stride=8) for r in range(8)]
+        largest, total = merged([(state_max[r, :], state_sum[r, :]) for r in rows])
+        ybuf[stage, half, y] = largest + jnp.log(total) * LOG2E
+        for device in y_near:
+            pltpu.make_async_remote_copy(
+                src_ref=ybuf.at[stage, half, y], dst_ref=ybuf.at[stage, half, y],
+                send_sem=ysend_sem.at[stage, half], recv_sem=yrecv_sem.at[stage, half],
+                device_id=device, device_id_type=MESH,
+            ).start()
+
+    def y_finish(stage, half):
+        got = ybuf.at[stage, half, pl.ds(0, YS - 1)]
+        pltpu.make_async_copy(got, got, yrecv_sem.at[stage, half]).wait()
+        largest, total = online([ybuf[stage, half, k] for k in range(YS)])
+        dbuf[pl.ds(half * HALF, HALF), :] = largest + jnp.log(total) * LOG2E
+
+    def frame_pass(half):
+        def body(b, _):
+            divisors = [dbuf[pl.ds(b * SPAN + u, 1), :] for u in range(SPAN)]
+            for g in range(GROUPS):
+                rows = pl.ds(8 * g, 8)
+                frame_max[b, rows, :], frame_sum[b, rows, :] = online(
+                    [energies[rows, at(b * SPAN + u)] - divisors[u] for u in range(SPAN)]
+                )
             return 0
 
-        lax.fori_loop(0, BLOCKS, body, 0, unroll=UNROLL)
-
-    def state_sum(terms, stage):
-        mbuf[...] = unfold(jnp.maximum)
-
-        def body(j, _):
-            scores = (terms + energies[:, at(j)]) - mbuf[pl.ds(j, 1), :]
-            fold[eight(j), :] = folded(jnp.exp2(scores), jnp.add)
-            return 0
-
-        lax.fori_loop(0, BLOCKS, body, 0, unroll=UNROLL)
-        ybuf[stage, y] = mbuf[...] + jnp.log(unfold(jnp.add)) * LOG2E
-
-    def y_send(stage):
-        for d in (2, 1, 3):
-            pltpu.make_async_remote_copy(
-                src_ref=ybuf.at[stage, y], dst_ref=ybuf.at[stage, y],
-                send_sem=ysend_sem.at[stage], recv_sem=yrecv_sem.at[stage],
-                device_id=(lax.rem(y + d, YS), f), device_id_type=MESH,
-            ).start()
-
-    def y_finish(stage):
-        got = ybuf.at[stage, pl.ds(0, YS - 1)]
-        pltpu.make_async_copy(got, got, yrecv_sem.at[stage]).wait()
-        parts = [ybuf[stage, k] for k in range(YS)]
-        largest = functools.reduce(jnp.maximum, parts)
-        total = functools.reduce(jnp.add, [jnp.exp2(part - largest) for part in parts])
-        dbuf[...] = largest + jnp.log(total) * LOG2E
-
-    def frame_sum(stage):
-        def greatest(j, most):
-            return jnp.maximum(most, energies[:, at(j)] - dbuf[pl.ds(j, 1), :])
-
-        most = lax.fori_loop(
-            0, BLOCKS, greatest, jnp.full((ROWS, LANES), -jnp.inf, jnp.float32), unroll=UNROLL
-        )
-        most = jnp.max(most, axis=1, keepdims=True)
-        shift = wide(most)
-
-        def add(j, total):
-            return total + jnp.exp2((energies[:, at(j)] - dbuf[pl.ds(j, 1), :]) - shift)
-
-        total = lax.fori_loop(0, BLOCKS, add, jnp.zeros((ROWS, LANES), jnp.float32), unroll=UNROLL)
-        total = jnp.sum(total, axis=1, keepdims=True)
+        lax.fori_loop(half * HALF // SPAN, (half + 1) * HALF // SPAN, body, 0)
+
+    frame_partners = sorted(
+        [(dx, dz, dc) for dx in range(XS) for dz in range(ZS) for dc in range(2)],
+        key=lambda k: min(k[0], XS - k[0]) + min(k[1], ZS - k[1]) + 0.5 * k[2],
+        reverse=True,
+    )[:-1]
+
+    def f_send(stage):
+        largest, total = merged([(frame_max[b], frame_sum[b]) for b in range(BLOCKS // SPAN)])
+        most = jnp.max(largest, axis=1, keepdims=True)
+        total = jnp.sum(total * jnp.exp2(largest - most), axis=1, keepdims=True)
         fbuf[stage, f] = to_row(most) + jnp.log(to_row(total)) * LOG2E
-
-    def hops(k):
-        dx, dz, dc = k
-        return min(dx, XS - dx) + min(dz, ZS - dz) + 0.5 * dc
-
-    frame_partners = sorted(
-        [(dx, dz, dc) for dx in range(XS) for dz in range(ZS) for dc in range(2)], key=hops, reverse=True
-    )[:-1]
-    x_at = [lax.rem(x + d, XS) * (2 * ZS) for d in range(XS)]
-    z_at = [lax.rem(z + d, ZS) * 2 for d in range(ZS)]
-    c_at = [core, 1 - core]
-
-    def f_send(stage):
         for dx, dz, dc in frame_partners:
             pltpu.make_async_remote_copy(
                 src_ref=fbuf.at[stage, f], dst_ref=fbuf.at[stage, f],
@@ -226,47 +222,68 @@
         largest = jnp.max(parts, axis=0)
         return -(largest + jnp.log(jnp.sum(jnp.exp2(parts - largest[None]), axis=0)) * LOG2E)
 
+    n_load.wait()
     log_counts = jnp.log(n_ref[...].astype(jnp.float32)) * LOG2E
-    terms = wide(to_col(log_counts))
-    for i in range(PARTS):
-        loads[i].wait()
-        scale_and_peak(terms, i * BLOCKS // PARTS, (i + 1) * BLOCKS // PARTS)
-    state_sum(terms, 0)
+    terms[...] = wide(to_col(log_counts))
+    share = BLOCKS // PARTS
+    loads[0].wait()
+    state_pass(0, share, scale=True)
+    loads[1].wait()
+    state_pass(share, 2 * share, scale=True)
+    pl.semaphore_wait(barrier, len(y_near + z_near + xc_near))
+    for device in z_near[:2]:
+        pl.semaphore_signal(z_ready, inc=1, device_id=device, device_id_type=MESH)
+    y_send(0, 0)
+    loads[2].wait()
+    state_pass(2 * share, 3 * share, scale=True)
+    loads[3].wait()
+    state_pass(3 * share, 4 * share, scale=True)
+    y_send(0, 1)
     bins_load.wait()
-    blocks = COLS // WIDE
-    pl.semaphore_wait(barrier, YS - 1 + FS - 1)
-    y_send(0)
-    count(0, blocks // 4)
-    y_finish(0)
-    frame_sum(0)
+    count(0, 6)
+    pl.semaphore_wait(z_ready, 2)
+    for device in xc_near:
+        pl.semaphore_signal(xc_ready, inc=1, device_id=device, device_id_type=MESH)
+    y_finish(0, 0)
+    frame_pass(0)
+    y_finish(0, 1)
+    frame_pass(1)
+    pl.semaphore_wait(xc_ready, len(xc_near))
     f_send(0)
-    count(blocks // 4, 3 * blocks // 4)
+    count(6, 18)
     free = f_finish(0)
 
-    terms = wide(to_col(log_counts + free))
-    peak(terms)
-    state_sum(terms, 1)
-    y_send(1)
-    count(3 * blocks // 4, blocks)
-    y_finish(1)
-    frame_sum(1)
+    terms[...] = wide(to_col(log_counts + free))
+    state_pass(0, HALF)
+    y_send(1, 0)
+    state_pass(HALF, BLOCKS)
+    y_send(1, 1)
+    count(18, 24)
+    y_finish(1, 0)
+    frame_pass(0)
+    y_finish(1, 1)
+    frame_pass(1)
     f_send(1)
+    count(24, COLS // WIDE)
     free = f_finish(1)
 
-    terms = wide(to_col(log_counts + free))
-    peak(terms)
-    state_sum(terms, 2)
-    y_send(2)
+    terms[...] = wide(to_col(log_counts + free))
+    state_pass(0, HALF)
+    y_send(2, 0)
+    state_pass(HALF, BLOCKS)
+    y_send(2, 1)
     free_col = to_col(free)
     factors = wide(free_col)
-    y_finish(2)
+    terms[...] = factors
 
     def weigh(j, _):
-        value = jnp.exp2((factors + energies[:, at(j)]) - dbuf[pl.ds(j, 1), :])
+        value = jnp.exp2((terms[...] + energies[:, at(j)]) - dbuf[pl.ds(j, 1), :])
         weights[:, at(j)] = value.astype(jnp.bfloat16)
         return 0
 
-    lax.fori_loop(0, BLOCKS, weigh, 0, unroll=UNROLL)
+    for half in range(2):
+        y_finish(2, half)
+        lax.fori_loop(half * HALF, (half + 1) * HALF, weigh, 0, unroll=SPAN)
 
     def offset(s):
         return 4 + (1 - 2 * lax.rem(s, 2)) * lax.div(s + 1, 2)
@@ -353,16 +370,17 @@
     for d in (2, 1, 3):
         near_copy(last, d).start()
 
+    leg_load.wait()
     leg_col = to_col(leg_ref[...].astype(jnp.float32))
     lane = lax.broadcasted_iota(jnp.int32, (ROWS, LANES), 1).astype(jnp.float32)
     table = (wide(leg_col) == lane).astype(jnp.float32)
     legbuf[y, 0:1] = jnp.sum(table * factors, axis=0, keepdims=True)
     legbuf[y, 1:2] = jnp.sum(table, axis=0, keepdims=True)
-    for d in (2, 1, 3):
+    for device in y_near:
         pltpu.make_async_remote_copy(
             src_ref=legbuf.at[y], dst_ref=legbuf.at[y],
             send_sem=legsend_sem, recv_sem=legrecv_sem,
-            device_id=(lax.rem(y + d, YS), f), device_id_type=MESH,
+            device_id=device, device_id_type=MESH,
         ).start()
     got = zrecv.at[pl.ds(0, FAR)]
     pltpu.make_async_copy(got, got, zrecv_sem).wait()
@@ -387,8 +405,9 @@
     out_ref[OWN : OWN + 8, :] = jnp.broadcast_to(to_row((free_col - own_mean) * LN2), (8, LANES))
 
     for stage in range(ITERS + 1):
-        sent = ybuf.at[stage, pl.ds(0, YS - 1)]
-        pltpu.make_async_copy(sent, sent, ysend_sem.at[stage]).wait()
+        for half in range(2):
+            sent = ybuf.at[stage, half, pl.ds(0, YS - 1)]
+            pltpu.make_async_copy(sent, sent, ysend_sem.at[stage, half]).wait()
     for stage in range(ITERS):
         sent = fbuf.at[stage, pl.ds(0, FS - 1)]
         pltpu.make_async_copy(sent, sent, fsend_sem.at[stage]).wait()
@@ -417,17 +436,22 @@
     both = pl.pallas_call(
         kernel,
         out_shape=jax.ShapeDtypeStruct((OWN + 8, LANES), f32),
-        in_specs=[hbm, vmem, vmem, hbm],
+        in_specs=[hbm] * 4,
         out_specs=vmem,
         scratch_shapes=[
             pltpu.VMEM((ROWS, COLS), f32),
+            pltpu.VMEM((1, LANES), jnp.int32),
+            pltpu.VMEM((1, LANES), jnp.int32),
             pltpu.VMEM((TYPES, PAIRS, COLS), jnp.int32),
             pltpu.VMEM((TYPES * BINS, COLS), jnp.bfloat16),
             pltpu.VMEM((ROWS, COLS), jnp.bfloat16),
+            pltpu.VMEM((ROWS, LANES), f32),
             pltpu.VMEM((BLOCKS * 8, LANES), f32),
+            pltpu.VMEM((BLOCKS * 8, LANES), f32),
+            pltpu.VMEM((BLOCKS // SPAN, ROWS, LANES), f32),
+            pltpu.VMEM((BLOCKS // SPAN, ROWS, LANES), f32),
             pltpu.VMEM((BLOCKS, LANES), f32),
-            pltpu.VMEM((BLOCKS, LANES), f32),
-            pltpu.VMEM((ITERS + 1, YS, BLOCKS, LANES), f32),
+            pltpu.VMEM((ITERS + 1, 2, YS, HALF, LANES), f32),
             pltpu.VMEM((ITERS, FS, 1, LANES), f32),
             pltpu.VMEM((YS, 2, LANES), f32),
             pltpu.VMEM((ZS, XS, 2, OWN, LANES), f32),
@@ -438,9 +462,12 @@
             pltpu.VMEM((FAR, OWN, LANES), f32),
             pltpu.VMEM((FAR, OWN, LANES), f32),
             dma((PARTS,)),
-            dma,
-            dma((ITERS + 1,)),
-            dma((ITERS + 1,)),
+            dma((2,)),
+            dma,
+            pltpu.SemaphoreType.REGULAR,
+            pltpu.SemaphoreType.REGULAR,
+            dma((ITERS + 1, 2)),
+            dma((ITERS + 1, 2)),
             dma((ITERS,)),
             dma((ITERS,)),
             dma,

time: 60.5 us -> 53.9 us (0.89)
  Pallas kernels: 59.6 us -> 53.1 us
    pallas_call x1, Pallas kernels: 58.3 us -> 51.7 us  [local(): pl.pallas_call(kernel, out_shape=jax.ShapeDtypeStruct((OWN + 8, LANES), f...]
where the time goes in v3:
time: 53.9 us; the launch traced here: 53.7 us
  Pallas kernels  53.1 us (99%)
  between operations  0.64 us (1%)
    pallas_call x1, Pallas kernels, local(): pl.pallas_call(kernel, out_shape=jax.ShapeDtypeStruct((OWN + 8, LANES), f...  51.7 us
    pallas_call x1, Pallas kernels, local(): pl.pallas_call(split, out_shape=(jax.ShapeDtypeStruct((OWN, LANES), f32),...  1.32 us

profile of v3, /device:TPU:1, one launch (start us, length us, event | category | flops | bytes accessed | tf_op | source)
XLA Modules:
  0.0 53.7 jit_solution(2441905714903527310)
XLA Ops:
  0.6 51.7 %reweight.1.both_ref = f32[32,128]{1,0:T(8,128)} custom-call(f32[128,8192]{1,0:T(8,128)} %e_hbm.1, s32[1,128]{1,0:T(1,128)} %bitcast.5, s32[1,128]{1,0:T(1,128)} %bitcast.6, s32[6,8,8192]{2,1,0:T(8,128)} %bitcast.4), custom_call_target="tpu_custom_call" | custom-call | tf_op jit(solution)/shard_map/reweight/pallas_call | solution.py:436
  52.4 1.3 %split.1 = (f32[24,128]{1,0:T(8,128)}, f32[1,128]{1,0:T(1,128)}) custom-call(f32[32,128]{1,0:T(8,128)} %reweight.1.both_ref), custom_call_target="tpu_custom_call" | custom-call | tf_op jit(solution)/shard_map/split/pallas_call | solution.py:494

commit v4 on v3

--- a/solution.py
+++ b/solution.py
@@ -29,7 +29,7 @@
 UNROLL = 4
 HALF = BLOCKS // 2
 SPAN = 8
-FAR = 3
+FAR = 2
 MESH = pl.DeviceIdType.MESH
 
 
@@ -94,9 +94,9 @@
 def kernel(
     e_hbm, n_hbm, leg_hbm, bins_hbm, out_ref,
     energies, n_ref, leg_ref, bins, counts, weights, terms, state_max, state_sum, frame_max, frame_sum, dbuf,
-    ybuf, fbuf, legbuf, part, crecv, xsend, xrecv, drecv, zsend, zrecv,
+    ybuf, fbuf, legbuf, part, crecv, xsend, xrecv, drecv, lrecv, zsend, zrecv,
     e_sem, small_sem, bins_sem, z_ready, xc_ready, ysend_sem, yrecv_sem, fsend_sem, frecv_sem, legsend_sem, legrecv_sem,
-    csend_sem, crecv_sem, xsend_sem, xrecv_sem, dsend_sem, drecv_sem, zsend_sem, zrecv_sem,
+    csend_sem, crecv_sem, xsend_sem, xrecv_sem, dsend_sem, drecv_sem, lsend_sem, lrecv_sem, zsend_sem, zrecv_sem,
 ):
     y = lax.axis_index("state")
     f = lax.axis_index("frame")
@@ -342,12 +342,17 @@
 
     lag = 5
 
-    def step(s, _):
+    last = ZS - 1
+
+    def product(s, frames):
         rows = pl.ds(pl.multiple_of(lax.rem(z + offset(s), ZS) * (XS * 2 * OWN), 32), XS * 2 * OWN)
         result = lax.dot_general(
-            counts[rows, :], weights[...], (((1,), (1,)), ((), ())), preferred_element_type=jnp.float32
+            counts[rows, frames], weights[:, frames], (((1,), (1,)), ((), ())), preferred_element_type=jnp.float32
         )
-        part[s] = result.reshape(XS, 2, OWN, LANES)
+        return result.reshape(XS, 2, OWN, LANES)
+
+    def step(s, _):
+        part[s] = product(s, slice(None))
         core_copy(s).start()
 
         @pl.when(jnp.logical_and(s >= 1, s <= FAR))
@@ -364,11 +369,17 @@
 
         return 0
 
-    lax.fori_loop(0, ZS, step, 0)
-    last = ZS - 1
-    core_post(last)
-    for d in (2, 1, 3):
-        near_copy(last, d).start()
+    lax.fori_loop(0, last, step, 0)
+    part[last] = product(last, slice(None))
+    near_post(last - 1)
+    last_partners = [(2, 1), (2, 0), (1, 1), (3, 1), (1, 0), (3, 0), (0, 1)]
+    for k, (dx, dc) in enumerate(last_partners):
+        c = c_at[dc]
+        pltpu.make_async_remote_copy(
+            src_ref=part.at[last, lax.rem(x + dx, XS), c], dst_ref=lrecv.at[k],
+            send_sem=lsend_sem, recv_sem=lrecv_sem,
+            device_id=(y, x_at[dx] + z_at[0] + c), device_id_type=MESH,
+        ).start()
 
     leg_load.wait()
     leg_col = to_col(leg_ref[...].astype(jnp.float32))
@@ -384,7 +395,7 @@
         ).start()
     got = zrecv.at[pl.ds(0, FAR)]
     pltpu.make_async_copy(got, got, zrecv_sem).wait()
-    total = xsend[last, x]
+    total = part[last, x, core]
     for s in range(FAR):
         total = total + zrecv[s]
     for s in range(FAR, last):
@@ -392,10 +403,9 @@
         pltpu.make_async_copy(got, got, drecv_sem.at[s - FAR]).wait()
         for d in range(XS):
             total = total + drecv[s - FAR, d]
-    got = drecv.at[last - FAR, pl.ds(1, XS - 1)]
-    pltpu.make_async_copy(got, got, drecv_sem.at[last - FAR]).wait()
-    for d in range(1, XS):
-        total = total + drecv[last - FAR, d]
+    pltpu.make_async_copy(lrecv, lrecv, lrecv_sem).wait()
+    for k in range(len(last_partners)):
+        total = total + lrecv[k]
     out_ref[0:OWN, :] = total * (BINS / PAIRS)
     got = legbuf.at[pl.ds(0, YS - 1)]
     pltpu.make_async_copy(got, got, legrecv_sem).wait()
@@ -415,10 +425,8 @@
     pltpu.make_async_copy(sent, sent, legsend_sem).wait()
     pltpu.make_async_copy(crecv, crecv, csend_sem).wait()
     pltpu.make_async_copy(xrecv, xrecv, xsend_sem).wait()
-    sent = drecv.at[pl.ds(0, last - FAR)]
-    pltpu.make_async_copy(sent, sent, dsend_sem).wait()
-    sent = drecv.at[last - FAR, pl.ds(1, XS - 1)]
-    pltpu.make_async_copy(sent, sent, dsend_sem).wait()
+    pltpu.make_async_copy(drecv, drecv, dsend_sem).wait()
+    pltpu.make_async_copy(lrecv, lrecv, lsend_sem).wait()
     sent = zrecv.at[pl.ds(0, FAR)]
     pltpu.make_async_copy(sent, sent, zsend_sem).wait()
 
@@ -455,10 +463,11 @@
             pltpu.VMEM((ITERS, FS, 1, LANES), f32),
             pltpu.VMEM((YS, 2, LANES), f32),
             pltpu.VMEM((ZS, XS, 2, OWN, LANES), f32),
-            pltpu.VMEM((ZS, XS, OWN, LANES), f32),
-            pltpu.VMEM((ZS, XS, OWN, LANES), f32),
+            pltpu.VMEM((ZS - 1, XS, OWN, LANES), f32),
+            pltpu.VMEM((ZS - 1, XS, OWN, LANES), f32),
             pltpu.VMEM((FAR, XS - 1, OWN, LANES), f32),
-            pltpu.VMEM((ZS - FAR, XS, OWN, LANES), f32),
+            pltpu.VMEM((ZS - 1 - FAR, XS, OWN, LANES), f32),
+            pltpu.VMEM((2 * XS - 1, OWN, LANES), f32),
             pltpu.VMEM((FAR, OWN, LANES), f32),
             pltpu.VMEM((FAR, OWN, LANES), f32),
             dma((PARTS,)),
@@ -473,11 +482,13 @@
             dma,
             dma,
             dma,
-            dma((ZS,)),
+            dma((ZS - 1,)),
             dma,
             dma((FAR,)),
             dma,
-            dma((ZS - FAR,)),
+            dma((ZS - 1 - FAR,)),
+            dma,
+            dma,
             dma,
             dma,
         ],

time: 53.9 us -> 53.6 us (level)
  no operation moved by 1% of the time
where the time goes in v4:
time: 53.6 us; the launch traced here: 53.5 us
  Pallas kernels  52.8 us (99%)
  between operations  0.64 us (1%)
    pallas_call x1, Pallas kernels, local(): pl.pallas_call(kernel, out_shape=jax.ShapeDtypeStruct((OWN + 8, LANES), f...  51.5 us
    pallas_call x1, Pallas kernels, local(): pl.pallas_call(split, out_shape=(jax.ShapeDtypeStruct((OWN, LANES), f32),...  1.32 us

profile of v4, /device:TPU:1, one launch (start us, length us, event | category | flops | bytes accessed | tf_op | source)
XLA Modules:
  0.0 53.5 jit_solution(5131487706597199882)
XLA Ops:
  0.6 51.5 %reweight.1.both_ref = f32[32,128]{1,0:T(8,128)} custom-call(f32[128,8192]{1,0:T(8,128)} %e_hbm.1, s32[1,128]{1,0:T(1,128)} %bitcast.5, s32[1,128]{1,0:T(1,128)} %bitcast.6, s32[6,8,8192]{2,1,0:T(8,128)} %bitcast.4), custom_call_target="tpu_custom_call" | custom-call | tf_op jit(solution)/shard_map/reweight/pallas_call | solution.py:444
  52.1 1.3 %split.1 = (f32[24,128]{1,0:T(8,128)}, f32[1,128]{1,0:T(1,128)}) custom-call(f32[32,128]{1,0:T(8,128)} %reweight.1.both_ref), custom_call_target="tpu_custom_call" | custom-call | tf_op jit(solution)/shard_map/split/pallas_call | solution.py:505

commit v5 on v4

--- a/solution.py
+++ b/solution.py
@@ -323,16 +323,20 @@
 
     def core_post(s):
         pltpu.make_async_copy(crecv.at[s], crecv.at[s], crecv_sem.at[s]).wait()
-        xsend[s] = part[s, :, core] + crecv[s]
 
     def far_post(s):
         core_post(s)
+        xsend[s, x] = part[s, x, core] + crecv[s, x]
         for d in (2, 1, 3):
+            to = lax.rem(x + d, XS)
+            xsend[s, to] = part[s, to, core] + crecv[s, to]
             x_copy(s, d).start()
 
     def near_post(s):
         core_post(s)
         for d in (2, 1, 3, 0):
+            to = lax.rem(x + d, XS)
+            xsend[s, to] = part[s, to, core] + crecv[s, to]
             near_copy(s, d).start()
 
     def x_post(s):
@@ -340,7 +344,7 @@
         zsend[s] = (xsend[s, x] + xrecv[s, 0]) + (xrecv[s, 1] + xrecv[s, 2])
         z_copy(s).start()
 
-    lag = 5
+    lag = 4
 
     last = ZS - 1
 
@@ -363,7 +367,7 @@
         def _():
             near_post(s - 1)
 
-        @pl.when(s >= lag)
+        @pl.when(jnp.logical_and(s >= lag, s < lag + FAR))
         def _():
             x_post(s - lag)
 
@@ -431,9 +435,15 @@
     pltpu.make_async_copy(sent, sent, zsend_sem).wait()
 
 
-def split(both_ref, rdf_ref, leg_ref):
-    rdf_ref[...] = both_ref[0:OWN, :]
-    leg_ref[...] = both_ref[OWN : OWN + 1, :]
+def split(both_ref, rdf_hbm, leg_hbm, sem):
+    copies = [
+        pltpu.make_async_copy(both_ref.at[pl.ds(0, OWN)], rdf_hbm, sem.at[0]),
+        pltpu.make_async_copy(both_ref.at[pl.ds(OWN, 1)], leg_hbm, sem.at[1]),
+    ]
+    for copy in copies:
+        copy.start()
+    for copy in copies:
+        copy.wait()
 
 
 def local(energies, sample_counts, state_leg, bin_index):
@@ -443,7 +453,7 @@
     dma = pltpu.SemaphoreType.DMA
     both = pl.pallas_call(
         kernel,
-        out_shape=jax.ShapeDtypeStruct((OWN + 8, LANES), f32),
+        out_shape=pltpu.VMEM((OWN + 8, LANES), f32),
         in_specs=[hbm] * 4,
         out_specs=vmem,
         scratch_shapes=[
@@ -506,7 +516,8 @@
         split,
         out_shape=(jax.ShapeDtypeStruct((OWN, LANES), f32), jax.ShapeDtypeStruct((1, LANES), f32)),
         in_specs=[vmem],
-        out_specs=(vmem, vmem),
+        out_specs=(hbm, hbm),
+        scratch_shapes=[dma((2,))],
         name="split",
     )(both)
     return rdf, leg_free.reshape(LANES)

time: 53.6 us -> 53.7 us (level)
  local copies, waits for them, and re-layouts: 0 us -> 0.59 us
    unnamed x0 -> x2, local copies, waits for them, and re-layouts: none -> 0.59 us
    pallas_call x1, Pallas kernels: 51.5 us -> 50.9 us  [local(): pl.pallas_call(kernel, out_shape=pltpu.VMEM((OWN + 8, LANES), f32), in_sp...]
where the time goes in v5:
time: 53.7 us; the launch traced here: 53.5 us
  Pallas kernels  52.3 us (97%)
  between operations  0.65 us (1%)
  local copies, waits for them, and re-layouts  0.59 us (1%)
    pallas_call x1, Pallas kernels, local(): pl.pallas_call(kernel, out_shape=pltpu.VMEM((OWN + 8, LANES), f32), in_sp...  50.9 us
    pallas_call x1, Pallas kernels, local(): pl.pallas_call(split, out_shape=(jax.ShapeDtypeStruct((OWN, LANES), f32),...  1.33 us

profile of v5, /device:TPU:1, one launch (start us, length us, event | category | flops | bytes accessed | tf_op | source)
XLA Modules:
  0.0 53.5 jit_solution(9613226241387692208)
XLA Ops:
  0.6 50.9 %reweight.1.both_ref = f32[32,128]{1,0:T(8,128)S(1)} custom-call(f32[128,8192]{1,0:T(8,128)} %e_hbm.1, s32[1,128]{1,0:T(1,128)} %bitcast.5, s32[1,128]{1,0:T(1,128)} %bitcast.6, s32[6,8,8192]{2,1,0:T(8,128)} %bitcast.4), custom_call_target="tpu_custom_call" | custom-call | tf_op jit(solution)/shard_map/reweight/pallas_call | solution.py:454
  51.6 0.0 copy-start
  51.6 0.6 %copy-done = f32[32,128]{1,0:T(8,128)} copy-done((f32[32,128]{1,0:T(8,128)}, f32[32,128]{1,0:T(8,128)S(1)}, u32[]{:S(2)}) %copy-start) | copy-done | bytes 16408
  52.2 1.3 %split.1 = (f32[24,128]{1,0:T(8,128)}, f32[1,128]{1,0:T(1,128)}) custom-call(f32[32,128]{1,0:T(8,128)} %copy-done), custom_call_target="tpu_custom_call" | custom-call | tf_op jit(solution)/shard_map/split/pallas_call | solution.py:515
Async XLA Ops:
  51.6 0.6 %copy-start = (f32[32,128]{1,0:T(8,128)}, f32[32,128]{1,0:T(8,128)S(1)}, u32[]{:S(2)}) copy-start(f32[32,128]{1,0:T(8,128)S(1)} %reweight.1.both_ref) | copy-start | bytes 49156
